TPU v7x, 32 devices: a whole 2x2x4 slice. The times are simulated.
32 devices in a mesh: groups: 2 (over x), shard: 16 (over z, y, core).
Axes of the slice: x: 2, y: 2, z: 4, core: 2. Of those that a mesh axis runs over, the one named last changes fastest.
Arguments:
- test_grads: bfloat16 [512, 8192], P(('groups', 'shard')), parts along dimension 0
- train_grads: bfloat16 [24576, 8192], P(('groups', 'shard')), parts along dimension 0
- candidates: int32 [512, 4], P(('groups', 'shard')), parts along dimension 0, may hold values from 0 to 15, all different within a row; in each aligned block of 16 rows (0 to 15, 16 to 31, ...) at most 4 rows name the same one
- owner: int32 [32], P('groups'), parts along dimension 0, may hold values from 0 to 15, each once
- cluster_sizes: int32 [32], P('groups'), parts along dimension 0, may hold values from 384 to 768, as said below
Outputs:
- influence: float32 [512, 4, 768], P(('groups', 'shard')), parts along dimension 0
There are 2 independent parts, one for each index of `groups`. A program takes and returns all parts, laid end to end along the dimension named above; each array names one. Nothing has to cross between parts.
Inputs may be any that keep to these rules, and one draw needn't show every extreme that they name: `candidates`: each row names 4 different clusters; among the test examples of one device no cluster is named by more than 4 of them. `owner`: each cluster is named exactly once. `cluster_sizes`: some cluster is full.
All inputs are finite; a program needn't handle non-finite values.
Results may differ from a plain program's by a relative error of at most 0.0003.
Values may be sent and summed in bfloat16 or wider, within the bound.
A program may use at most 128 MiB of HBM per device.

v0:
```python
import jax
import jax.numpy as jnp
from jax import lax
from jax.sharding import PartitionSpec as P

EPS = 1e-06


def shards(test_grads, train_grads, candidates, owner, cluster_sizes):
    peer_count = lax.axis_size("shard")
    my_index = lax.axis_index("shard")
    capacity, proj_width = train_grads.shape
    tests_here, per_test = candidates.shape
    entries = tests_here * per_test
    slot_count = max(2, (entries + peer_count - 1) // peer_count)
    cluster_ids = jnp.arange(owner.shape[0], dtype=jnp.int32)
    owned = owner == my_index
    my_size = jnp.sum(jnp.where(owned, cluster_sizes, 0))
    widened = train_grads.astype(jnp.float32)
    row_norms = jnp.sqrt(jnp.mean(widened * widened, axis=1) + EPS)
    live_rows = jnp.arange(capacity, dtype=jnp.int32) < my_size

    def destinations(cand_block):
        flattened = cand_block.reshape(-1)
        owner_of = jnp.sum(
            jnp.where(flattened[:, None] == cluster_ids[None, :], owner[None, :], 0), axis=1
        )
        order = jnp.arange(flattened.shape[0], dtype=jnp.int32)
        earlier = (owner_of[:, None] == owner_of[None, :]) & (order[None, :] < order[:, None])
        position = jnp.sum(earlier.astype(jnp.int32), axis=1)
        return (owner_of, position)

    owner_of, position = destinations(candidates)
    slot_index = owner_of * slot_count + position
    everyone = lax.all_gather(candidates, "shard", axis=0, tiled=True)
    raw_dot = jnp.einsum(
        "...k,rk->...r",
        lax.all_gather(test_grads, "shard", axis=0, tiled=True),
        train_grads,
        preferred_element_type=jnp.float32,
    )
    all_scores = jnp.where(live_rows, raw_dot / row_norms, 0.0)
    blocks = everyone.reshape(peer_count, tests_here, per_test)
    all_owner, all_position = jax.vmap(destinations)(blocks)
    source_ids = jnp.arange(peer_count, dtype=jnp.int32)
    test_of = (
        source_ids[:, None] * tests_here + jnp.arange(entries, dtype=jnp.int32)[None, :] // per_test
    )
    matches = (all_owner == my_index)[:, None, :] & (
        all_position[:, None, :] == jnp.arange(slot_count, dtype=jnp.int32)[None, :, None]
    )
    chosen_test = jnp.sum(jnp.where(matches, test_of[:, None, :], 0), axis=2)
    filled = jnp.any(matches, axis=2)
    picked = jnp.take(all_scores, chosen_test.reshape(-1), axis=0).reshape(
        peer_count, slot_count, capacity
    )
    answers = jnp.where(filled[:, :, None], picked, 0.0)
    returned = lax.all_to_all(answers, "shard", split_axis=0, concat_axis=0, tiled=True)
    scores = jnp.take(returned.reshape(peer_count * slot_count, capacity), slot_index, axis=0)
    scores = scores.reshape(tests_here, per_test, capacity)
    sizes_picked = jnp.sum(
        jnp.where(
            candidates[:, :, None] == cluster_ids[None, None, :], cluster_sizes[None, None, :], 0
        ),
        axis=2,
    )
    valid_count = jnp.sum(sizes_picked, axis=1).astype(jnp.float32)
    meansq = jnp.sum(scores * scores, axis=(1, 2)) / valid_count
    return scores / jnp.sqrt(meansq + EPS)[:, None, None]


def solution(mesh):
    in_specs = (
        P(("groups", "shard"), None),
        P(("groups", "shard"), None),
        P(("groups", "shard"), None),
        P("groups"),
        P("groups"),
    )
    out_specs = P(("groups", "shard"), None, None)
    return jax.shard_map(shards, mesh=mesh, in_specs=in_specs, out_specs=out_specs, check_vma=False)
```

profile of v0, /device:TPU:0, one launch (start us, length us, event | category | flops | bytes accessed | tf_op | source)
XLA Modules:
  0.0 99.7 jit_solution(15154001654175937103)
XLA Ops:
  6.5 0.0 all-gather.3.cloned.1.call-start
  6.5 0.7 all-gather.3.cloned.1.call-update
  7.3 0.8 copy.16
  8.0 23.5 %all-gather = s32[16,16,4]{1,2,0:T(4,128)S(1)} all-gather(s32[1,16,4]{1,2,0:T(4,128)} %bitcast.11), channel_id=1, replica_groups=mesh['groups'=2,'shard'=16] {'shard'}, dimensions={0}, use_global_device_ids=true | all-gather | bytes 4352 | tf_op jit(solution)/shard_map/all_gather | solution.py:35
  31.5 0.1 copy.21
  31.6 0.1 copy.22
  31.7 0.8 select_reduce_fusion
  32.5 0.5 convert_reduce_fusion
  33.0 0.1 broadcast_add_fusion
  33.0 0.2 select_reduce_fusion.2
  33.2 0.1 copy.25
  33.3 0.1 reshape.195
  33.4 0.1 copy.24
  33.5 0.2 fusion.2
  33.7 0.1 copy.23
  33.8 0.1 eq.98
  33.8 0.7 select_reduce_fusion.3
  34.6 0.2 convert_reduce_fusion.1
  34.8 0.1 add.110
  34.9 0.1 copy.17
  35.0 0.1 copy.20
  35.1 1.3 %fusion.3 = s32[]{:T(128)} fusion(s32[16]{0:T(128)} %param.9, s32[16]{0:T(128)} %param.8, s32[]{:T(128)S(6)} %axis_index.12), kind=kLoop, calls=%fused_computation.40 | loop fusion | flops 47 | bytes 136 | tf_op jit(solution)/shard_map/reduce_sum | solution.py:18
  36.4 0.6 iota_compare_fusion.5
  37.1 7.6 %multiply_reduce_fusion = f32[768]{0:T(1024)S(1)} fusion(bf16[768,8192]{1,0:T(8,128)(2,1)} %param.6), kind=kLoop, calls=%fused_computation.2 | loop fusion | flops 18873600 | bytes 12585984 | tf_op jit(solution)/shard_map/reduce_sum | solution.py:20
  44.7 0.0 copy-start
  44.7 0.0 copy-start.1
  44.7 18.2 %all-gather.3.cloned.1.call-done = bf16[256,8192]{1,0:T(8,128)(2,1)} async-done(((bf16[16,8192]{1,0:T(8,128)(2,1)}), bf16[256,8192]{1,0:T(8,128)(2,1)}) %all-gather.3.cloned.1.call-update) | async-done | bytes 4194320 | tf_op jit(solution)/shard_map/all_gather | solution.py:38
  62.9 13.8 %fusion = f32[256,768]{1,0:T(8,128)S(1)} fusion(bf16[256,8192]{1,0:T(8,128)(2,1)} %all-gather.3.cloned.1.call-done, bf16[768,8192]{1,0:T(8,128)(2,1)} %param.6, f32[768]{0:T(1024)S(1)} %add_sqrt_fusion, pred[768]{0:T(1024)(128)(4,1)S(1)} %iota_compare_fusion.5), kind=kOutput, calls=%fused_computation.4 | convolution fusion | flops 3221618688 | bytes 17567488 | tf_op jit(solution)/shard_map/...k,rk->...r/dot_general | solution.py:36
  76.7 0.7 gather_fusion
  77.4 0.1 gather.13
  77.5 0.8 select_select_fusion
  78.3 3.5 %all-to-all-start = ((f32[16,4,768]{2,1,0:T(4,128)}), f32[16,4,768]{2,1,0:T(4,128)S(1)}, u32[]{:S(2)}, u32[]{:S(2)}) async-start(f32[16,4,768]{2,1,0:T(4,128)} %select_select_fusion), calls=%async_computation | async-start | bytes 393216 | tf_op jit(solution)/shard_map/all_to_all | solution.py:58
  81.8 0.0 copy-done
  81.9 0.0 copy-done.1
  81.9 0.2 select_reduce_fusion.1
  82.1 8.7 %all-to-all-done = f32[16,4,768]{2,1,0:T(4,128)S(1)} async-done(((f32[16,4,768]{2,1,0:T(4,128)}), f32[16,4,768]{2,1,0:T(4,128)S(1)}, u32[]{:S(2)}, u32[]{:S(2)}) %all-to-all-start) | async-done | bytes 196640 | tf_op jit(solution)/shard_map/all_to_all | solution.py:58
  90.8 0.1 reshape.196
  90.9 0.7 gather_fusion.1
  91.5 0.1 gather.15
  91.6 0.2 multiply_reduce_fusion.1
  91.8 0.1 reduce_sum.100
  91.9 0.1 reduce_sum.101
  92.0 0.8 select_divide_fusion
  (13 shorter events, 0.1 us)
Async XLA Ops:
  6.5 56.4 %all-gather.3.cloned.1.call-start = ((), (), s32[]{:S(2)}) async-start(), calls=%async_computation.1 | async-start | bytes 4456448 | tf_op jit(solution)/shard_map/all_gather | solution.py:38
  44.7 37.2 %copy-start = (s32[16,4]{0,1:T(4,128)S(1)}, s32[16,4]{0,1:T(4,128)}, u32[]{:S(2)}) copy-start(s32[16,4]{0,1:T(4,128)} %param.7) | copy-start | bytes 772
  44.7 37.2 %copy-start.1 = (s32[16]{0:T(128)S(1)}, s32[16]{0:T(128)}, u32[]{:S(2)}) copy-start(s32[16]{0:T(128)} %param.9) | copy-start | bytes 196
  78.3 12.5 %all-to-all-start = ((f32[16,4,768]{2,1,0:T(4,128)}), f32[16,4,768]{2,1,0:T(4,128)S(1)}, u32[]{:S(2)}, u32[]{:S(2)}) async-start(f32[16,4,768]{2,1,0:T(4,128)} %select_select_fusion), calls=%async_computation | async-start | bytes 393216 | tf_op jit(solution)/shard_map/all_to_all | solution.py:58
Sparse Core Ops, SparseCore 0:
  9.5 53.3 all-gather.2
where the time goes:
time: 100 us; the launch traced here: 99.7 us
  waiting for transfers between devices  27.6 us (28%)
  blocking collectives  23.5 us (24%)
  other arithmetic  14.4 us (14%)
  matrix products  13.8 us (14%)
  between operations  13.5 us (14%)
  starting transfers between devices  3.52 us (4%)
  local copies, waits for them, and re-layouts  3.32 us (3%)
    all_gather x1, blocking collectives, shards(): everyone = lax.all_gather(candidates, 'shard', axis=0, tiled=True)  23.5 us
    all_gather x1, waiting for transfers between devices, shards(): lax.all_gather(test_grads, 'shard', axis=0, tiled=True)  18.2 us
    dot_general x1, matrix products, shards(): jnp.einsum('...k,rk->...r', lax.all_gather(test_grads, 'shard', axis=0, t...  13.8 us
    all_to_all x1, waiting for transfers between devices, shards(): lax.all_to_all(answers, 'shard', split_axis=0, concat_axis=0, tiled=True)  8.73 us
    reduce_sum x1, other arithmetic, shards(): row_norms = jnp.sqrt(jnp.mean(widened * widened, axis=1) + EPS)  7.61 us
    all_to_all x1, starting transfers between devices, shards(): lax.all_to_all(answers, 'shard', split_axis=0, concat_axis=0, tiled=True)  3.52 us
  transfers between devices with their start and end apart: 2, of which 2 were waited for; matrix products, arithmetic and copies ran while one was open for 14% of the time, Pallas kernels for 0%

commit v1 on v0

v1 whole, which is shorter than its diff:
```python
import functools

import jax
import jax.numpy as jnp
from jax import lax
from jax.experimental import pallas as pl
from jax.experimental.pallas import tpu as pltpu
from jax.sharding import PartitionSpec as P

EPS = 1e-06
CHUNKS = 4
TILE = 16
F32 = jnp.float32
BF16 = jnp.bfloat16


def iota(shape, dim):
    return lax.broadcasted_iota(jnp.int32, shape, dim)


def dot_nn(a, b):
    return lax.dot_general(a, b, (((1,), (0,)), ((), ())), preferred_element_type=F32)


def dot_nt(a, b):
    return lax.dot_general(a, b, (((1,), (1,)), ((), ())), preferred_element_type=F32)


def log2(n):
    assert n & (n - 1) == 0
    return n.bit_length() - 1


def onehot(condition):
    return jnp.where(condition, 1.0, 0.0).astype(BF16)


def kernel(
    peers,
    slots,
    test_ref,
    train_ref,
    cand_ref,
    owner_ref,
    size_ref,
    out_ref,
    train_v,
    send_v,
    recv_v,
    square_v,
    score_v,
    answer_v,
    back_v,
    train_sem,
    send_sem,
    recv_sem,
    answer_sem,
    back_sem,
):
    tests, per_test = cand_ref.shape
    clusters = owner_ref.shape[1]
    chunks, capacity, chunk_width = train_v.shape
    subs = TILE // slots
    width = chunk_width // subs
    half = capacity // 2
    me = lax.axis_index("shard")

    def load(c):
        return pltpu.make_async_copy(
            train_ref.at[:, pl.ds(c * chunk_width, chunk_width)], train_v.at[c], train_sem.at[c]
        )

    def scatter(c, off):
        to = lax.rem(me + off, peers)
        return pltpu.make_async_remote_copy(
            src_ref=send_v.at[c, to],
            dst_ref=recv_v.at[c, me],
            send_sem=send_sem.at[c, off],
            recv_sem=recv_sem.at[c, off],
            device_id={"shard": to},
            device_id_type=pl.DeviceIdType.MESH,
        )

    def reply(off):
        to = lax.rem(me + off, peers)
        return pltpu.make_async_remote_copy(
            src_ref=answer_v.at[to],
            dst_ref=back_v.at[me],
            send_sem=answer_sem.at[off],
            recv_sem=back_sem.at[off],
            device_id={"shard": to},
            device_id_type=pl.DeviceIdType.MESH,
        )

    for c in range(chunks):
        load(c).start()

    barrier = pltpu.get_barrier_semaphore()

    @pl.loop(1, peers)
    def _(off):
        pl.semaphore_signal(
            barrier,
            inc=1,
            device_id={"shard": lax.rem(me + off, peers)},
            device_id_type=pl.DeviceIdType.MESH,
        )

    named = [
        onehot(cand_ref[:, j : j + 1] == iota((tests, clusters), 1)) for j in range(per_test)
    ]
    owned = onehot(owner_ref[...] == iota((peers, clusters), 0))
    holder = [dot_nt(chosen, owned) for chosen in named]
    asks = functools.reduce(jnp.add, holder)
    before = onehot(iota((tests, tests), 1) < iota((tests, tests), 0))
    place = dot_nn(before, asks.astype(BF16)) + 1.0
    taken = (asks * place).astype(BF16)

    rows = peers * TILE
    spread = onehot((iota((rows, peers), 0) >> log2(TILE)) == iota((rows, peers), 1))
    tile = onehot((iota((tests, subs * tests), 1) & (tests - 1)) == iota((tests, subs * tests), 0))
    wanted = dot_nn(dot_nt(spread, taken).astype(BF16), tile)
    row = iota((rows, subs * tests), 0) & (TILE - 1)
    column = iota((rows, subs * tests), 1)
    same_block = (row >> log2(slots)) == (column >> log2(tests))
    pick = onehot(same_block & (wanted == ((row & (slots - 1)) + 1).astype(F32)))

    for c in range(chunks):
        blocks = [
            test_ref[:, c * chunk_width + q * width : c * chunk_width + (q + 1) * width]
            for q in range(subs)
        ]
        block = dot_nn(pick, jnp.concatenate(blocks, axis=0)).astype(BF16)
        send_v[c] = block.reshape(peers, TILE, width)

    pl.semaphore_wait(barrier, peers - 1)

    for c in range(chunks):

        @pl.loop(1, peers)
        def _(off):
            scatter(c, off).start()

        recv_v[c, me] = send_v[c, me]

    step = 64
    square_v[...] = jnp.zeros_like(square_v)

    @pl.loop(0, chunks)
    def _(c):
        load(c).wait()

        @pl.loop(0, capacity // step)
        def _(b):
            at = pl.ds(pl.multiple_of(b * step, step), step)
            total = square_v[at, :]
            for k in range(chunk_width // 128):
                x = train_v[c, at, k * 128 : (k + 1) * 128].astype(F32)
                total += x * x
            square_v[at, :] = total

    mean = jnp.sum(square_v[...].T, axis=0, keepdims=True) / (chunks * chunk_width)
    mine = jnp.where(owner_ref[...] == me, size_ref[...], 0)
    my_size = jnp.sum(mine.astype(F32), axis=1, keepdims=True)
    live = iota((1, capacity), 1).astype(F32) < my_size
    scale = lax.rsqrt(mean + EPS)

    @pl.loop(0, chunks)
    def _(c):
        @pl.loop(1, peers)
        def _(off):
            scatter(c, off).wait_recv()

        got = recv_v[c].reshape(rows, width)
        which = (iota((rows, width), 0) & (TILE - 1)) >> log2(slots)
        spaced = jnp.concatenate(
            [jnp.where(which == q, got, jnp.zeros_like(got)) for q in range(subs)], axis=1
        )
        part = dot_nt(spaced, train_v[c])

        @pl.when(c == 0)
        def _():
            score_v[...] = part

        @pl.when(c != 0)
        def _():
            score_v[...] += part

    full = score_v[...].reshape(peers, 2, 8, capacity)
    full = (full[:, 0] + full[:, 1]).reshape(peers * 8, capacity)
    turn = slots
    shifted = iota((peers * 8, capacity), 0) & 7
    while turn < 8:
        ahead = pltpu.roll(full, peers * 8 - turn, 0)
        behind = pltpu.roll(full, turn, 0)
        full = full + jnp.where((shifted & turn) == 0, ahead, behind)
        turn *= 2
    full = jnp.where(live, full * scale, 0.0)
    sub = iota((peers * 8, half), 0) & 7
    packed = jnp.where(sub < 4, full[:, :half], full[:, half:])
    answer_v[...] = packed.reshape(peers, 8, half)

    @pl.loop(1, peers)
    def _(off):
        reply(off).start()

    back_v[me] = answer_v[me]

    wide = peers * 8
    spread_back = onehot((iota((wide, peers), 0) >> 3) == iota((wide, peers), 1))
    spot = iota((tests, wide), 1) & 7
    valid = jnp.zeros((tests, 1), F32)
    left, right = [], []
    for j in range(per_test):
        at = dot_nt((holder[j] * place).astype(BF16), spread_back)
        left.append(onehot(at == (spot + 1).astype(F32)))
        right.append(onehot(at == (spot - 3).astype(F32)))
        sizes = jnp.where(named[j] > 0, size_ref[...].astype(F32), 0.0)
        valid += jnp.sum(sizes, axis=1, keepdims=True)
    left = jnp.where(iota((per_test * tests, wide), 1) & 7 < 4, jnp.concatenate(left, axis=0), 0)
    right = jnp.where(
        iota((per_test * tests, wide), 1) & 7 >= 4, jnp.concatenate(right, axis=0), 0
    )
    select = jnp.concatenate([left, right], axis=0).astype(BF16)

    @pl.loop(1, peers)
    def _(off):
        reply(off).wait_recv()

    rest = back_v[...].reshape(wide, half)
    chosen = jnp.zeros((2 * per_test * tests, half), F32)
    for _ in range(3):
        term = rest.astype(BF16)
        chosen += dot_nn(select, term)
        rest = rest - term.astype(F32)

    entries = per_test * tests
    energy = jnp.zeros((tests, 1), F32)
    for j in range(per_test):
        for h in range(2):
            x = chosen[h * entries + j * tests : h * entries + (j + 1) * tests]
            energy += jnp.sum(x * x, axis=1, keepdims=True)
    factor = lax.rsqrt(energy / valid + EPS)
    for j in range(per_test):
        for h in range(2):
            x = chosen[h * entries + j * tests : h * entries + (j + 1) * tests]
            out_ref[:, j * capacity + h * half : j * capacity + (h + 1) * half] = x * factor

    @pl.loop(1, peers)
    def _(off):
        for c in range(chunks):
            scatter(c, off).wait_send()
        reply(off).wait_send()


def shards(test_grads, train_grads, candidates, owner, cluster_sizes):
    peers = lax.axis_size("shard")
    capacity, depth = train_grads.shape
    tests, per_test = candidates.shape
    slots = max(2, -(-tests * per_test // peers))
    subs = TILE // slots
    chunk = depth // CHUNKS
    half = capacity // 2
    vmem = pl.BlockSpec(memory_space=pltpu.VMEM)
    out = pl.pallas_call(
        functools.partial(kernel, peers, slots),
        out_shape=jax.ShapeDtypeStruct((tests, per_test * capacity), F32),
        in_specs=[vmem, pl.BlockSpec(memory_space=pl.ANY), vmem, vmem, vmem],
        out_specs=vmem,
        scratch_shapes=[
            pltpu.VMEM((CHUNKS, capacity, chunk), BF16),
            pltpu.VMEM((CHUNKS, peers, TILE, chunk // subs), BF16),
            pltpu.VMEM((CHUNKS, peers, TILE, chunk // subs), BF16),
            pltpu.VMEM((capacity, 128), F32),
            pltpu.VMEM((peers * TILE, capacity), F32),
            pltpu.VMEM((peers, 8, half), F32),
            pltpu.VMEM((peers, 8, half), F32),
            pltpu.SemaphoreType.DMA((CHUNKS,)),
            pltpu.SemaphoreType.DMA((CHUNKS, peers)),
            pltpu.SemaphoreType.DMA((CHUNKS, peers)),
            pltpu.SemaphoreType.DMA((peers,)),
            pltpu.SemaphoreType.DMA((peers,)),
        ],
        compiler_params=pltpu.CompilerParams(
            collective_id=0, has_side_effects=True, vmem_limit_bytes=56 * 1024 * 1024
        ),
    )(test_grads, train_grads, candidates, owner[None, :], cluster_sizes[None, :])
    return out.reshape(tests, per_test, capacity)


def solution(mesh):
    in_specs = (
        P(("groups", "shard"), None),
        P(("groups", "shard"), None),
        P(("groups", "shard"), None),
        P("groups"),
        P("groups"),
    )
    out_specs = P(("groups", "shard"), None, None)
    return jax.shard_map(shards, mesh=mesh, in_specs=in_specs, out_specs=out_specs, check_vma=False)
```

time: 100 us -> 43.1 us (0.43)
  Pallas kernels: 0 us -> 39.9 us
  waiting for transfers between devices: 27.6 us -> 0 us
  blocking collectives: 23.5 us -> 0 us
  other arithmetic: 14.4 us -> 0 us
  matrix products: 13.8 us -> 0 us
  between operations: 13.5 us -> 0.01 us
  starting transfers between devices: 3.52 us -> 0 us
    pallas_call x0 -> x1, Pallas kernels: none -> 39.9 us  [shards(): pl.pallas_call(functools.partial(kernel, peers, slots), out_shape=jax.Sha...]
    all_gather x1 -> x0, blocking collectives: 23.5 us -> none  [shards(): everyone = lax.all_gather(candidates, 'shard', axis=0, tiled=True)]
    all_gather x1 -> x0, waiting for transfers between devices: 18.2 us -> none  [shards(): lax.all_gather(test_grads, 'shard', axis=0, tiled=True)]
    dot_general x1 -> x0, matrix products: 13.8 us -> none  [shards(): jnp.einsum('...k,rk->...r', lax.all_gather(test_grads, 'shard', axis=0, t...]
    reduce_sum x10 -> x0, other arithmetic: 11.8 us -> none  [the longest x1 7.61 us: shards(): row_norms = jnp.sqrt(jnp.mean(widened * widened, axis=1) + EPS)]
    all_to_all x1 -> x0, waiting for transfers between devices: 8.73 us -> none  [shards(): lax.all_to_all(answers, 'shard', split_axis=0, concat_axis=0, tiled=True)]
    all_to_all x1 -> x0, starting transfers between devices: 3.52 us -> none  [shards(): lax.all_to_all(answers, 'shard', split_axis=0, concat_axis=0, tiled=True)]
    reshape x2 -> x1, local copies, waits for them, and re-layouts: 0.17 us -> 1.7 us  [shards(): return out.reshape(tests, per_test, capacity)]
  transfers between devices with their start and end apart: 2 -> 0, of which waited for: 2 -> 0; matrix products, arithmetic and copies ran while one was open for 14% -> 0% of each run, Pallas kernels for 0% -> 0%
where the time goes in v1:
time: 43.1 us; the launch traced here: 42.9 us
  Pallas kernels  39.9 us (93%)
  local copies, waits for them, and re-layouts  3.05 us (7%)
    pallas_call x1, Pallas kernels, shards(): pl.pallas_call(functools.partial(kernel, peers, slots), out_shape=jax.Sha...  39.9 us
    reshape x1, local copies, waits for them, and re-layouts, shards(): return out.reshape(tests, per_test, capacity)  1.7 us
    unnamed x1, local copies, waits for them, and re-layouts  1.35 us

profile of v1, /device:TPU:0, one launch (start us, length us, event | category | flops | bytes accessed | tf_op | source)
XLA Modules:
  0.0 42.9 jit_solution(3012764627078105033)
XLA Ops:
  0.0 1.4 %copy.6.cand_ref = s32[16,4]{1,0:T(8,128)} copy(s32[16,4]{0,1:T(4,128)} %param.7) | data formatting | bytes 512 | tf_op args[2]
  1.4 39.9 %shard_map.55 = f32[16,3072]{1,0:T(8,128)} custom-call(bf16[16,8192]{1,0:T(8,128)(2,1)} %test_ref.1, bf16[768,8192]{1,0:T(8,128)(2,1)} %train_ref.1, s32[16,4]{1,0:T(8,128)} %copy.6.cand_ref, s32[1,16]{1,0:T(1,128)} %bitcast.2, s32[1,16]{1,0:T(1,128)} %bitcast.3), custom_call_target="tpu_custom_call" | custom-call | tf_op jit(solution)/shard_map/pallas_call | solution.py:265
  41.2 1.7 %reshape.3 = f32[16,4,768]{2,1,0:T(4,128)} reshape(f32[16,3072]{1,0:T(8,128)} %shard_map.55) | data formatting | bytes 393216 | tf_op jit(solution)/shard_map/reshape | solution.py:288

commit v2 on v1

v2 whole, which is shorter than its diff:
```python
import functools

import jax
import jax.numpy as jnp
from jax import lax
from jax.experimental import pallas as pl
from jax.experimental.pallas import tpu as pltpu
from jax.sharding import PartitionSpec as P

EPS = 1e-06
CHUNKS = 4
TILE = 16
SLAB = 4
F32 = jnp.float32
BF16 = jnp.bfloat16


def iota(shape, dim):
    return lax.broadcasted_iota(jnp.int32, shape, dim)


def dot_nn(a, b):
    return lax.dot_general(a, b, (((1,), (0,)), ((), ())), preferred_element_type=F32)


def dot_nt(a, b):
    return lax.dot_general(a, b, (((1,), (1,)), ((), ())), preferred_element_type=F32)


def log2(n):
    assert n & (n - 1) == 0
    return n.bit_length() - 1


def owner_wide(peers):
    return -(-peers // 128) * 128


def onehot(condition):
    return jnp.where(condition, 1.0, 0.0).astype(BF16)


def kernel(
    peers,
    slots,
    test_ref,
    train_ref,
    cand_ref,
    owner_ref,
    size_ref,
    out_ref,
    train_v,
    line_v,
    taken_v,
    pick_v,
    stage_v,
    recv_v,
    square_v,
    score_v,
    answer_v,
    back_v,
    train_sem,
    line_sem,
    down_sem,
    up_sem,
    taken_sem,
    told_sem,
    stage_sem,
    recv_sem,
    answer_sem,
    back_sem,
):
    per_test, tests = cand_ref.shape
    clusters = owner_ref.shape[1]
    chunks, capacity, chunk_width = train_v.shape
    subs = TILE // slots
    width = chunk_width // subs
    half = capacity // 2
    length = peers // SLAB
    me = lax.axis_index("shard")
    level = lax.div(me, SLAB)
    member = lax.rem(me, SLAB)
    rows = SLAB * TILE

    def remote(src, dst, sent, got, to):
        return pltpu.make_async_remote_copy(
            src_ref=src,
            dst_ref=dst,
            send_sem=sent,
            recv_sem=got,
            device_id={"shard": to},
            device_id_type=pl.DeviceIdType.MESH,
        )

    def load(c):
        return pltpu.make_async_copy(
            train_ref.at[:, pl.ds(c * chunk_width, chunk_width)], train_v.at[c], train_sem.at[c]
        )

    def down(s, c):
        at = line_v.at[s, c]
        return remote(at, at, down_sem.at[s, c], line_sem.at[s, c], lax.rem(me - SLAB + peers, peers))

    def up(s, c):
        at = line_v.at[s, c]
        return remote(at, at, up_sem.at[s, c], line_sem.at[s, c], lax.rem(me + SLAB, peers))

    def tell(off):
        to = lax.rem(me + off * SLAB, peers)
        at = taken_v.at[level]
        return remote(at, at, taken_sem.at[off], told_sem.at[level], to)

    def told(s):
        at = taken_v.at[s]
        return remote(at, at, taken_sem.at[0], told_sem.at[s], lax.rem(me + SLAB, peers))

    def hand(s, c, off):
        to = lax.rem(member + off, SLAB)
        return remote(
            stage_v.at[s, c, to],
            recv_v.at[s, c, member],
            stage_sem.at[s, c, off],
            recv_sem.at[s, c, off],
            level * SLAB + to,
        )

    def reply(s, g):
        to = s * SLAB + g
        return remote(answer_v.at[s, g], back_v.at[me], answer_sem.at[to], back_sem.at[me], to)

    def came(p):
        at = back_v.at[p]
        return remote(at, at, answer_sem.at[p], back_sem.at[p], lax.rem(me + 1, peers))

    for c in range(chunks):
        load(c).start()

    barrier = pltpu.get_barrier_semaphore()

    @pl.loop(1, peers)
    def _(off):
        pl.semaphore_signal(
            barrier,
            inc=1,
            device_id={"shard": lax.rem(me + off, peers)},
            device_id_type=pl.DeviceIdType.MESH,
        )

    for c in range(chunks):
        line_v[level, c] = test_ref[:, c * chunk_width : (c + 1) * chunk_width]

    eye = onehot(iota((tests, tests), 0) == iota((tests, tests), 1))
    cand = dot_nt(eye, cand_ref[...].astype(F32).astype(BF16))
    ids = iota((tests, clusters), 1).astype(F32)
    named = [onehot(cand[:, j : j + 1] == ids) for j in range(per_test)]
    owned = onehot(owner_ref[...] == iota((owner_wide(peers), clusters), 0))
    holder = [dot_nt(chosen, owned) for chosen in named]
    asks = functools.reduce(jnp.add, holder)
    before = onehot(iota((tests, tests), 1) < iota((tests, tests), 0))
    place = dot_nn(before, asks.astype(BF16)) + 1.0
    taken_v[level] = (asks * place).astype(BF16)

    def choose(s):
        wide = owner_wide(peers)
        spread = onehot(
            (iota((rows, wide), 0) >> log2(TILE)) + level * SLAB == iota((rows, wide), 1)
        )
        tile = onehot(
            (iota((tests, subs * tests), 1) & (tests - 1)) == iota((tests, subs * tests), 0)
        )
        wanted = dot_nn(dot_nt(spread, taken_v[s]).astype(BF16), tile)
        row = iota((rows, subs * tests), 0) & (TILE - 1)
        column = iota((rows, subs * tests), 1)
        same_block = (row >> log2(slots)) == (column >> log2(tests))
        return onehot(same_block & (wanted == ((row & (slots - 1)) + 1).astype(F32)))

    def deal(s, c, pick):
        blocks = [line_v[s, c, :, q * width : (q + 1) * width] for q in range(subs)]
        block = dot_nn(pick, jnp.concatenate(blocks, axis=0)).astype(BF16)
        stage_v[s, c] = block.reshape(SLAB, TILE, width)
        for off in range(1, SLAB):
            hand(s, c, off).start()
        recv_v[s, c, member] = stage_v[s, c, member]

    pl.semaphore_wait(barrier, peers - 1)

    @pl.loop(0, chunks)
    def _(c):
        @pl.when(level > 0)
        def _():
            down(level, c).start()

        @pl.when(level < length - 1)
        def _():
            up(level, c).start()

    @pl.loop(1, length)
    def _(off):
        tell(off).start()

    pick_v[0] = choose(level)

    @pl.loop(0, chunks)
    def _(c):
        deal(level, c, pick_v[0])

    step = 64
    square_v[...] = jnp.zeros_like(square_v)

    @pl.loop(0, chunks)
    def _(c):
        load(c).wait()

        @pl.loop(0, capacity // step)
        def _(b):
            at = pl.ds(pl.multiple_of(b * step, step), step)
            total = square_v[at, :]
            for k in range(chunk_width // 128):
                x = train_v[c, at, k * 128 : (k + 1) * 128].astype(F32)
                total += x * x
            square_v[at, :] = total

    mean = jnp.sum(square_v[...].T, axis=0, keepdims=True) / (chunks * chunk_width)
    mine = jnp.where(owner_ref[...] == me, size_ref[...], 0)
    my_size = jnp.sum(mine.astype(F32), axis=1, keepdims=True)
    live = iota((1, capacity), 1).astype(F32) < my_size
    scale = lax.rsqrt(mean + EPS)

    def multiply(s, c, way):
        for off in range(1, SLAB):
            hand(s, c, off).wait_recv()
        got = recv_v[s, c].reshape(rows, width)
        which = (iota((rows, width), 0) & (TILE - 1)) >> log2(slots)
        spaced = jnp.concatenate(
            [jnp.where(which == q, got, jnp.zeros_like(got)) for q in range(subs)], axis=1
        )
        part = dot_nt(spaced, train_v[c])

        @pl.when(c == 0)
        def _():
            score_v[way] = part

        @pl.when(c != 0)
        def _():
            score_v[way] += part

        @pl.when(c == chunks - 1)
        def _():
            answer(s, way)

    def answer(s, way):
        full = score_v[way].reshape(SLAB, 2, 8, capacity)
        full = (full[:, 0] + full[:, 1]).reshape(SLAB * 8, capacity)
        turn = slots
        at = iota((SLAB * 8, capacity), 0) & 7
        while turn < 8:
            ahead = pltpu.roll(full, SLAB * 8 - turn, 0)
            behind = pltpu.roll(full, turn, 0)
            full = full + jnp.where((at & turn) == 0, ahead, behind)
            turn *= 2
        full = jnp.where(live, full * scale, 0.0)
        sub = iota((SLAB * 8, half), 0) & 7
        packed = jnp.where(sub < 4, full[:, :half], full[:, half:])
        answer_v[s] = packed.reshape(SLAB, 8, half)
        for g in range(SLAB):

            @pl.when(s * SLAB + g != me)
            def _():
                reply(s, g).start()

        @pl.when(s == level)
        def _():
            back_v[me] = answer_v[s, member]

    @pl.loop(0, length * chunks + 1)
    def _(t):
        far, c = lax.div(t, chunks), lax.rem(t, chunks)
        for way in range(2):
            s = level - far if way else level + far
            there = (far > 0) & (far < length) & (s >= 0) & (s < length)

            @pl.when(there)
            def _():
                if way:
                    up(s, c).wait_recv()

                    @pl.when(level < length - 1)
                    def _():
                        up(s, c).start()

                else:
                    down(s, c).wait_recv()

                    @pl.when(level > 0)
                    def _():
                        down(s, c).start()

                @pl.when(c == 0)
                def _():
                    told(s).wait_recv()
                    pick_v[way] = choose(s)

                deal(s, c, pick_v[way])

        last = t - 1
        far, c = lax.div(last + chunks, chunks) - 1, lax.rem(last + chunks, chunks)
        for way in range(2):
            s = level - far if way else level + far
            there = (t > 0) & (s >= 0) & (s < length)
            if way:
                there = there & (far > 0)

            @pl.when(there)
            def _():
                multiply(s, c, way)

    wide = peers * 8
    spread_back = onehot(
        (iota((wide, owner_wide(peers)), 0) >> 3) == iota((wide, owner_wide(peers)), 1)
    )
    spot = iota((tests, wide), 1) & 7
    valid = jnp.zeros((tests, 1), F32)
    left, right = [], []
    for j in range(per_test):
        at = dot_nt((holder[j] * place).astype(BF16), spread_back)
        left.append(onehot(at == (spot + 1).astype(F32)))
        right.append(onehot(at == (spot - 3).astype(F32)))
        sizes = jnp.where(named[j] > 0, size_ref[...].astype(F32), 0.0)
        valid += jnp.sum(sizes, axis=1, keepdims=True)
    left = jnp.where(iota((per_test * tests, wide), 1) & 7 < 4, jnp.concatenate(left, axis=0), 0)
    right = jnp.where(
        iota((per_test * tests, wide), 1) & 7 >= 4, jnp.concatenate(right, axis=0), 0
    )
    select = jnp.concatenate([left, right], axis=0).astype(BF16)

    @pl.loop(1, peers)
    def _(off):
        came(lax.rem(me + off, peers)).wait_recv()

    rest = back_v[...].reshape(wide, half)
    chosen = jnp.zeros((2 * per_test * tests, half), F32)
    for _ in range(3):
        term = rest.astype(BF16)
        chosen += dot_nn(select, term)
        rest = rest - term.astype(F32)

    entries = per_test * tests
    energy = jnp.zeros((tests, 1), F32)
    for j in range(per_test):
        for h in range(2):
            x = chosen[h * entries + j * tests : h * entries + (j + 1) * tests]
            energy += jnp.sum(x * x, axis=1, keepdims=True)
    factor = lax.rsqrt(energy / valid + EPS)
    for j in range(per_test):
        for h in range(2):
            x = chosen[h * entries + j * tests : h * entries + (j + 1) * tests]
            out_ref[:, j, h * half : (h + 1) * half] = x * factor

    @pl.loop(0, length)
    def _(s):
        @pl.loop(0, chunks)
        def _(c):
            @pl.when((level > 0) & (s >= level))
            def _():
                down(s, c).wait_send()

            @pl.when((level < length - 1) & (s <= level))
            def _():
                up(s, c).wait_send()

            for off in range(1, SLAB):
                hand(s, c, off).wait_send()

        for g in range(SLAB):

            @pl.when(s * SLAB + g != me)
            def _():
                reply(s, g).wait_send()

    @pl.loop(1, length)
    def _(off):
        tell(off).wait_send()


def shards(test_grads, train_grads, candidates, owner, cluster_sizes):
    peers = lax.axis_size("shard")
    capacity, depth = train_grads.shape
    tests, per_test = candidates.shape
    slots = max(2, -(-tests * per_test // peers))
    subs = TILE // slots
    chunk = depth // CHUNKS
    half = capacity // 2
    length = peers // SLAB
    vmem = pl.BlockSpec(memory_space=pltpu.VMEM)
    out = pl.pallas_call(
        functools.partial(kernel, peers, slots),
        out_shape=jax.ShapeDtypeStruct((tests, per_test, capacity), F32),
        in_specs=[vmem, pl.BlockSpec(memory_space=pl.ANY), vmem, vmem, vmem],
        out_specs=vmem,
        scratch_shapes=[
            pltpu.VMEM((CHUNKS, capacity, chunk), BF16),
            pltpu.VMEM((length, CHUNKS, tests, chunk), BF16),
            pltpu.VMEM((length, tests, owner_wide(peers)), BF16),
            pltpu.VMEM((2, SLAB * TILE, subs * tests), BF16),
            pltpu.VMEM((length, CHUNKS, SLAB, TILE, chunk // subs), BF16),
            pltpu.VMEM((length, CHUNKS, SLAB, TILE, chunk // subs), BF16),
            pltpu.VMEM((capacity, 128), F32),
            pltpu.VMEM((2, SLAB * TILE, capacity), F32),
            pltpu.VMEM((length, SLAB, 8, half), F32),
            pltpu.VMEM((peers, 8, half), F32),
            pltpu.SemaphoreType.DMA((CHUNKS,)),
            pltpu.SemaphoreType.DMA((length, CHUNKS)),
            pltpu.SemaphoreType.DMA((length, CHUNKS)),
            pltpu.SemaphoreType.DMA((length, CHUNKS)),
            pltpu.SemaphoreType.DMA((length,)),
            pltpu.SemaphoreType.DMA((length,)),
            pltpu.SemaphoreType.DMA((length, CHUNKS, SLAB)),
            pltpu.SemaphoreType.DMA((length, CHUNKS, SLAB)),
            pltpu.SemaphoreType.DMA((peers,)),
            pltpu.SemaphoreType.DMA((peers,)),
        ],
        compiler_params=pltpu.CompilerParams(
            collective_id=0, has_side_effects=True, vmem_limit_bytes=56 * 1024 * 1024
        ),
    )(test_grads, train_grads, candidates.T, owner[None, :], cluster_sizes[None, :])
    return out


def solution(mesh):
    in_specs = (
        P(("groups", "shard"), None),
        P(("groups", "shard"), None),
        P(("groups", "shard"), None),
        P("groups"),
        P("groups"),
    )
    out_specs = P(("groups", "shard"), None, None)
    return jax.shard_map(shards, mesh=mesh, in_specs=in_specs, out_specs=out_specs, check_vma=False)
```

time: 43.1 us -> 49.3 us (1.14)
  Pallas kernels: 39.9 us -> 47.5 us
  local copies, waits for them, and re-layouts: 3.05 us -> 1.62 us
    pallas_call x1, Pallas kernels: 39.9 us -> 47.5 us  [shards(): pl.pallas_call(functools.partial(kernel, peers, slots), out_shape=jax.Sha...]
    reshape x1 -> x0, local copies, waits for them, and re-layouts: 1.7 us -> none  [shards(): return out.reshape(tests, per_test, capacity)]
where the time goes in v2:
time: 49.3 us; the launch traced here: 49.2 us
  Pallas kernels  47.5 us (96%)
  local copies, waits for them, and re-layouts  1.62 us (3%)
    pallas_call x1, Pallas kernels, shards(): pl.pallas_call(functools.partial(kernel, peers, slots), out_shape=jax.Sha...  47.5 us
    unnamed x1, local copies, waits for them, and re-layouts  1.62 us

profile of v2, /device:TPU:0, one launch (start us, length us, event | category | flops | bytes accessed | tf_op | source)
XLA Modules:
  0.0 49.2 jit_solution(8091294997297497572)
XLA Ops:
  0.0 47.5 %shard_map.55 = f32[16,4,768]{2,1,0:T(4,128)} custom-call(bf16[16,8192]{1,0:T(8,128)(2,1)} %test_ref.1, bf16[768,8192]{1,0:T(8,128)(2,1)} %train_ref.1, s32[4,16]{1,0:T(4,128)} %bitcast.3, s32[1,16]{1,0:T(1,128)} %bitcast.4, s32[1,16]{1,0:T(1,128)} %bitcast.5), custom_call_target="tpu_custom_call" | custom-call | tf_op jit(solution)/shard_map/pallas_call | solution.py:395
  47.5 1.6 %copy.7 = f32[16,4,768]{2,1,0:T(4,128)} copy(f32[16,4,768]{2,1,0:T(4,128)} %shard_map.55) | data formatting | bytes 393216

commit v3 on v1

--- a/solution.py
+++ b/solution.py
@@ -57,7 +57,7 @@
     answer_sem,
     back_sem,
 ):
-    tests, per_test = cand_ref.shape
+    per_test, tests = cand_ref.shape
     clusters = owner_ref.shape[1]
     chunks, capacity, chunk_width = train_v.shape
     subs = TILE // slots
@@ -106,9 +106,10 @@
             device_id_type=pl.DeviceIdType.MESH,
         )
 
-    named = [
-        onehot(cand_ref[:, j : j + 1] == iota((tests, clusters), 1)) for j in range(per_test)
-    ]
+    eye = onehot(iota((tests, tests), 0) == iota((tests, tests), 1))
+    cand = dot_nt(eye, cand_ref[...].astype(F32).astype(BF16))
+    ids = iota((tests, clusters), 1).astype(F32)
+    named = [onehot(cand[:, j : j + 1] == ids) for j in range(per_test)]
     owned = onehot(owner_ref[...] == iota((peers, clusters), 0))
     holder = [dot_nt(chosen, owned) for chosen in named]
     asks = functools.reduce(jnp.add, holder)
@@ -244,7 +245,7 @@
     for j in range(per_test):
         for h in range(2):
             x = chosen[h * entries + j * tests : h * entries + (j + 1) * tests]
-            out_ref[:, j * capacity + h * half : j * capacity + (h + 1) * half] = x * factor
+            out_ref[:, j, h * half : (h + 1) * half] = x * factor
 
     @pl.loop(1, peers)
     def _(off):
@@ -264,7 +265,7 @@
     vmem = pl.BlockSpec(memory_space=pltpu.VMEM)
     out = pl.pallas_call(
         functools.partial(kernel, peers, slots),
-        out_shape=jax.ShapeDtypeStruct((tests, per_test * capacity), F32),
+        out_shape=jax.ShapeDtypeStruct((tests, per_test, capacity), F32),
         in_specs=[vmem, pl.BlockSpec(memory_space=pl.ANY), vmem, vmem, vmem],
         out_specs=vmem,
         scratch_shapes=[
@@ -284,8 +285,8 @@
         compiler_params=pltpu.CompilerParams(
             collective_id=0, has_side_effects=True, vmem_limit_bytes=56 * 1024 * 1024
         ),
-    )(test_grads, train_grads, candidates, owner[None, :], cluster_sizes[None, :])
-    return out.reshape(tests, per_test, capacity)
+    )(test_grads, train_grads, candidates.T, owner[None, :], cluster_sizes[None, :])
+    return out
 
 
 def solution(mesh):

time: 43.1 us -> 41.7 us (0.968)
  local copies, waits for them, and re-layouts: 3.05 us -> 1.62 us
    reshape x1 -> x0, local copies, waits for them, and re-layouts: 1.7 us -> none  [shards(): return out.reshape(tests, per_test, capacity)]
where the time goes in v3:
time: 41.7 us; the launch traced here: 41.5 us
  Pallas kernels  39.9 us (96%)
  local copies, waits for them, and re-layouts  1.62 us (4%)
    pallas_call x1, Pallas kernels, shards(): pl.pallas_call(functools.partial(kernel, peers, slots), out_shape=jax.Sha...  39.9 us
    unnamed x1, local copies, waits for them, and re-layouts  1.62 us

profile of v3, /device:TPU:0, one launch (start us, length us, event | category | flops | bytes accessed | tf_op | source)
XLA Modules:
  0.0 41.5 jit_solution(948588751122565676)
XLA Ops:
  0.0 39.9 %shard_map.55 = f32[16,4,768]{2,1,0:T(4,128)} custom-call(bf16[16,8192]{1,0:T(8,128)(2,1)} %test_ref.1, bf16[768,8192]{1,0:T(8,128)(2,1)} %train_ref.1, s32[4,16]{1,0:T(4,128)} %bitcast.3, s32[1,16]{1,0:T(1,128)} %bitcast.4, s32[1,16]{1,0:T(1,128)} %bitcast.5), custom_call_target="tpu_custom_call" | custom-call | tf_op jit(solution)/shard_map/pallas_call | solution.py:266
  39.9 1.6 %copy.7 = f32[16,4,768]{2,1,0:T(4,128)} copy(f32[16,4,768]{2,1,0:T(4,128)} %shard_map.55) | data formatting | bytes 393216

commit v4 on v3

--- a/solution.py
+++ b/solution.py
@@ -29,6 +29,10 @@
 def log2(n):
     assert n & (n - 1) == 0
     return n.bit_length() - 1
+
+
+def padded(peers):
+    return -(-peers // 128) * 128
 
 
 def onehot(condition):
@@ -45,13 +49,20 @@
     size_ref,
     out_ref,
     train_v,
+    far_v,
+    taken_v,
     send_v,
+    relay_v,
     recv_v,
     square_v,
     score_v,
     answer_v,
     back_v,
     train_sem,
+    raw_sem,
+    far_sem,
+    taken_sem,
+    told_sem,
     send_sem,
     recv_sem,
     answer_sem,
@@ -63,6 +74,7 @@
     subs = TILE // slots
     width = chunk_width // subs
     half = capacity // 2
+    wide_peers = padded(peers)
     me = lax.axis_index("shard")
 
     def load(c):
@@ -70,14 +82,39 @@
             train_ref.at[:, pl.ds(c * chunk_width, chunk_width)], train_v.at[c], train_sem.at[c]
         )
 
-    def scatter(c, off):
-        to = lax.rem(me + off, peers)
+    near = peers // 2
+    base = lax.div(me, near) * near
+    member = lax.rem(me, near)
+    partner = lax.rem(me + near, peers)
+
+    def deal(which, c, off):
+        to = lax.rem(member + off, near)
         return pltpu.make_async_remote_copy(
-            src_ref=send_v.at[c, to],
-            dst_ref=recv_v.at[c, me],
-            send_sem=send_sem.at[c, off],
-            recv_sem=recv_sem.at[c, off],
-            device_id={"shard": to},
+            src_ref=(relay_v if which else send_v).at[c, to],
+            dst_ref=recv_v.at[c, partner if which else me],
+            send_sem=send_sem.at[which, c, off],
+            recv_sem=recv_sem.at[which, c, off],
+            device_id={"shard": base + to},
+            device_id_type=pl.DeviceIdType.MESH,
+        )
+
+    def cross(c):
+        return pltpu.make_async_remote_copy(
+            src_ref=test_ref.at[:, pl.ds(c * chunk_width, chunk_width)],
+            dst_ref=far_v.at[c],
+            send_sem=raw_sem.at[c],
+            recv_sem=far_sem.at[c],
+            device_id={"shard": partner},
+            device_id_type=pl.DeviceIdType.MESH,
+        )
+
+    def tell():
+        return pltpu.make_async_remote_copy(
+            src_ref=taken_v.at[0],
+            dst_ref=taken_v.at[1],
+            send_sem=taken_sem,
+            recv_sem=told_sem,
+            device_id={"shard": partner},
             device_id_type=pl.DeviceIdType.MESH,
         )
 
@@ -110,45 +147,64 @@
     cand = dot_nt(eye, cand_ref[...].astype(F32).astype(BF16))
     ids = iota((tests, clusters), 1).astype(F32)
     named = [onehot(cand[:, j : j + 1] == ids) for j in range(per_test)]
-    owned = onehot(owner_ref[...] == iota((peers, clusters), 0))
+    owned = onehot(owner_ref[...] == iota((wide_peers, clusters), 0))
     holder = [dot_nt(chosen, owned) for chosen in named]
     asks = functools.reduce(jnp.add, holder)
     before = onehot(iota((tests, tests), 1) < iota((tests, tests), 0))
     place = dot_nn(before, asks.astype(BF16)) + 1.0
-    taken = (asks * place).astype(BF16)
-
-    rows = peers * TILE
-    spread = onehot((iota((rows, peers), 0) >> log2(TILE)) == iota((rows, peers), 1))
-    tile = onehot((iota((tests, subs * tests), 1) & (tests - 1)) == iota((tests, subs * tests), 0))
-    wanted = dot_nn(dot_nt(spread, taken).astype(BF16), tile)
-    row = iota((rows, subs * tests), 0) & (TILE - 1)
-    column = iota((rows, subs * tests), 1)
-    same_block = (row >> log2(slots)) == (column >> log2(tests))
-    pick = onehot(same_block & (wanted == ((row & (slots - 1)) + 1).astype(F32)))
-
-    for c in range(chunks):
-        blocks = [
-            test_ref[:, c * chunk_width + q * width : c * chunk_width + (q + 1) * width]
-            for q in range(subs)
-        ]
+    taken_v[0] = (asks * place).astype(BF16)
+
+    dealt = near * TILE
+
+    def choose(taken):
+        spread = onehot(
+            (iota((dealt, wide_peers), 0) >> log2(TILE)) + base == iota((dealt, wide_peers), 1)
+        )
+        tile = onehot(
+            (iota((tests, subs * tests), 1) & (tests - 1)) == iota((tests, subs * tests), 0)
+        )
+        wanted = dot_nn(dot_nt(spread, taken).astype(BF16), tile)
+        row = iota((dealt, subs * tests), 0) & (TILE - 1)
+        column = iota((dealt, subs * tests), 1)
+        same_block = (row >> log2(slots)) == (column >> log2(tests))
+        return onehot(same_block & (wanted == ((row & (slots - 1)) + 1).astype(F32)))
+
+    def select_rows(pick, chunk):
+        blocks = [chunk[:, q * width : (q + 1) * width] for q in range(subs)]
         block = dot_nn(pick, jnp.concatenate(blocks, axis=0)).astype(BF16)
-        send_v[c] = block.reshape(peers, TILE, width)
+        return block.reshape(near, TILE, width)
+
+    pick = choose(taken_v[0])
+    for c in range(chunks):
+        send_v[c] = select_rows(pick, test_ref[:, c * chunk_width : (c + 1) * chunk_width])
 
     pl.semaphore_wait(barrier, peers - 1)
 
-    for c in range(chunks):
-
-        @pl.loop(1, peers)
+    tell().start()
+    for c in range(chunks):
+        cross(c).start()
+    for c in range(chunks):
+
+        @pl.loop(1, near)
         def _(off):
-            scatter(c, off).start()
-
-        recv_v[c, me] = send_v[c, me]
-
+            deal(0, c, off).start()
+
+        recv_v[c, me] = send_v[c, member]
+
+    tell().wait_recv()
+    pick = choose(taken_v[1])
+    square_v[...] = jnp.zeros_like(square_v)
     step = 64
-    square_v[...] = jnp.zeros_like(square_v)
-
-    @pl.loop(0, chunks)
-    def _(c):
+
+    for c in range(chunks):
+        cross(c).wait_recv()
+        relay_v[c] = select_rows(pick, far_v[c])
+
+        @pl.loop(1, near)
+        def _(off):
+            deal(1, c, off).start()
+
+        recv_v[c, partner] = relay_v[c, member]
         load(c).wait()
 
         @pl.loop(0, capacity // step)
@@ -168,10 +224,12 @@
 
     @pl.loop(0, chunks)
     def _(c):
-        @pl.loop(1, peers)
+        @pl.loop(1, near)
         def _(off):
-            scatter(c, off).wait_recv()
-
+            deal(0, c, off).wait_recv()
+            deal(1, c, off).wait_recv()
+
+        rows = peers * TILE
         got = recv_v[c].reshape(rows, width)
         which = (iota((rows, width), 0) & (TILE - 1)) >> log2(slots)
         spaced = jnp.concatenate(
@@ -208,7 +266,9 @@
     back_v[me] = answer_v[me]
 
     wide = peers * 8
-    spread_back = onehot((iota((wide, peers), 0) >> 3) == iota((wide, peers), 1))
+    spread_back = onehot(
+        (iota((wide, wide_peers), 0) >> 3) == iota((wide, wide_peers), 1)
+    )
     spot = iota((tests, wide), 1) & 7
     valid = jnp.zeros((tests, 1), F32)
     left, right = [], []
@@ -249,9 +309,17 @@
 
     @pl.loop(1, peers)
     def _(off):
+        reply(off).wait_send()
+
+    @pl.loop(1, near)
+    def _(off):
         for c in range(chunks):
-            scatter(c, off).wait_send()
-        reply(off).wait_send()
+            deal(0, c, off).wait_send()
+            deal(1, c, off).wait_send()
+
+    for c in range(chunks):
+        cross(c).wait_send()
+    tell().wait_send()
 
 
 def shards(test_grads, train_grads, candidates, owner, cluster_sizes):
@@ -262,6 +330,7 @@
     subs = TILE // slots
     chunk = depth // CHUNKS
     half = capacity // 2
+    near = peers // 2
     vmem = pl.BlockSpec(memory_space=pltpu.VMEM)
     out = pl.pallas_call(
         functools.partial(kernel, peers, slots),
@@ -270,15 +339,22 @@
         out_specs=vmem,
         scratch_shapes=[
             pltpu.VMEM((CHUNKS, capacity, chunk), BF16),
-            pltpu.VMEM((CHUNKS, peers, TILE, chunk // subs), BF16),
+            pltpu.VMEM((CHUNKS, tests, chunk), BF16),
+            pltpu.VMEM((2, tests, padded(peers)), BF16),
+            pltpu.VMEM((CHUNKS, near, TILE, chunk // subs), BF16),
+            pltpu.VMEM((CHUNKS, near, TILE, chunk // subs), BF16),
             pltpu.VMEM((CHUNKS, peers, TILE, chunk // subs), BF16),
             pltpu.VMEM((capacity, 128), F32),
             pltpu.VMEM((peers * TILE, capacity), F32),
             pltpu.VMEM((peers, 8, half), F32),
             pltpu.VMEM((peers, 8, half), F32),
             pltpu.SemaphoreType.DMA((CHUNKS,)),
-            pltpu.SemaphoreType.DMA((CHUNKS, peers)),
-            pltpu.SemaphoreType.DMA((CHUNKS, peers)),
+            pltpu.SemaphoreType.DMA((CHUNKS,)),
+            pltpu.SemaphoreType.DMA((CHUNKS,)),
+            pltpu.SemaphoreType.DMA,
+            pltpu.SemaphoreType.DMA,
+            pltpu.SemaphoreType.DMA((2, CHUNKS, near)),
+            pltpu.SemaphoreType.DMA((2, CHUNKS, near)),
             pltpu.SemaphoreType.DMA((peers,)),
             pltpu.SemaphoreType.DMA((peers,)),
         ],

time: 41.7 us -> 36.3 us (0.87)
  Pallas kernels: 39.9 us -> 34.5 us
    pallas_call x1, Pallas kernels: 39.9 us -> 34.5 us  [shards(): pl.pallas_call(functools.partial(kernel, peers, slots), out_shape=jax.Sha...]
where the time goes in v4:
time: 36.3 us; the launch traced here: 36.2 us
  Pallas kernels  34.5 us (95%)
  local copies, waits for them, and re-layouts  1.62 us (4%)
    pallas_call x1, Pallas kernels, shards(): pl.pallas_call(functools.partial(kernel, peers, slots), out_shape=jax.Sha...  34.5 us
    unnamed x1, local copies, waits for them, and re-layouts  1.62 us

profile of v4, /device:TPU:0, one launch (start us, length us, event | category | flops | bytes accessed | tf_op | source)
XLA Modules:
  0.0 36.2 jit_solution(17183100906608732655)
XLA Ops:
  0.0 34.5 %shard_map.55 = f32[16,4,768]{2,1,0:T(4,128)} custom-call(bf16[16,8192]{1,0:T(8,128)(2,1)} %test_ref.1, bf16[768,8192]{1,0:T(8,128)(2,1)} %train_ref.1, s32[4,16]{1,0:T(4,128)} %bitcast.3, s32[1,16]{1,0:T(1,128)} %bitcast.4, s32[1,16]{1,0:T(1,128)} %bitcast.5), custom_call_target="tpu_custom_call" | custom-call | tf_op jit(solution)/shard_map/pallas_call | solution.py:335
  34.5 1.6 %copy.7 = f32[16,4,768]{2,1,0:T(4,128)} copy(f32[16,4,768]{2,1,0:T(4,128)} %shard_map.55) | data formatting | bytes 393216

commit v5 on v4

--- a/solution.py
+++ b/solution.py
@@ -8,7 +8,7 @@
 from jax.sharding import PartitionSpec as P
 
 EPS = 1e-06
-CHUNKS = 4
+CHUNKS = 8
 TILE = 16
 F32 = jnp.float32
 BF16 = jnp.bfloat16

time: 36.3 us -> 37.7 us (1.039)
  Pallas kernels: 34.5 us -> 35.8 us
    pallas_call x1, Pallas kernels: 34.5 us -> 35.8 us  [shards(): pl.pallas_call(functools.partial(kernel, peers, slots), out_shape=jax.Sha...]
where the time goes in v5:
time: 37.7 us; the launch traced here: 37.5 us
  Pallas kernels  35.8 us (95%)
  local copies, waits for them, and re-layouts  1.62 us (4%)
    pallas_call x1, Pallas kernels, shards(): pl.pallas_call(functools.partial(kernel, peers, slots), out_shape=jax.Sha...  35.8 us
    unnamed x1, local copies, waits for them, and re-layouts  1.62 us

profile of v5, /device:TPU:0, one launch (start us, length us, event | category | flops | bytes accessed | tf_op | source)
XLA Modules:
  0.0 37.5 jit_solution(836126421078394389)
XLA Ops:
  0.0 35.8 %shard_map.55 = f32[16,4,768]{2,1,0:T(4,128)} custom-call(bf16[16,8192]{1,0:T(8,128)(2,1)} %test_ref.1, bf16[768,8192]{1,0:T(8,128)(2,1)} %train_ref.1, s32[4,16]{1,0:T(4,128)} %bitcast.3, s32[1,16]{1,0:T(1,128)} %bitcast.4, s32[1,16]{1,0:T(1,128)} %bitcast.5), custom_call_target="tpu_custom_call" | custom-call | tf_op jit(solution)/shard_map/pallas_call | solution.py:335
  35.9 1.6 %copy.7 = f32[16,4,768]{2,1,0:T(4,128)} copy(f32[16,4,768]{2,1,0:T(4,128)} %shard_map.55) | data formatting | bytes 393216
